TPU v7x, 256 devices: a whole 4x4x8 slice. The times are simulated.
256 devices in a mesh: dp: 4 (over x), ctx: 16 (over z, core), head: 4 (over y).
Axes of the slice: x: 4, y: 4, z: 8, core: 2. Of those that a mesh axis runs over, the one named last changes fastest.
Arguments:
- inputs: bfloat16 [4, 2048, 4096], P('dp', 'ctx', 'head'), may hold values from -6 to 6
- step_rate: float32 [4, 2048, 4096], P('dp', 'ctx', 'head'), may hold values from 0 to 12
- key_rows: bfloat16 [4, 2048, 16], P('dp', 'ctx'), may hold values from -5 to 5
- query_rows: bfloat16 [4, 2048, 16], P('dp', 'ctx'), may hold values from -1.5 to 1.5
- grad_out: bfloat16 [4, 2048, 4096], P('dp', 'ctx', 'head'), may hold values from -6 to 6
Outputs:
- grad_inputs: bfloat16 [4, 2048, 4096], P('dp', ('ctx', 'head'))
- grad_rate: bfloat16 [4, 2048, 4096], P('dp', ('ctx', 'head'))
- grad_keys: float32 [4, 2048, 16], P('dp', ('ctx', 'head'))
- grad_queries: float32 [4, 2048, 16], P('dp', ('ctx', 'head'))
All inputs are finite; a program needn't handle non-finite values.
Results may differ from a plain program's by a relative error of at most 0.0018.
Values may be sent and summed in bfloat16 or wider, within the bound.
A program may use at most 64 MiB of HBM per device.

v0:
```python
import jax
import jax.numpy as jnp
from jax import lax
from jax.experimental import pallas as pl
from jax.experimental.pallas import tpu as pltpu
from jax.sharding import PartitionSpec as P

MESH = pl.DeviceIdType.MESH
F32 = jnp.float32
BF16 = jnp.bfloat16

SEG = 8
LEN = 16
N = 16
LANES = 128
PAIRS = 4
WIDE = 256
CTX = 16
TOKENS = SEG * LEN


def kernel(
    heads,
    x_ref, rate_ref, k_ref, q_ref, g_ref,
    oi_ref, or_ref, ok_ref, oq_ref,
    kT, k2T, qT, knT,
    x32, g32, r32,
    stepP, uP, gP, xP, invP,
    sumP, sumL, sumB,
    preP, preL, postP, postB,
    send1, recv1, send2, recv2,
    sIn, gIn, kpS,
    accQ, accK, accN,
    outI, outR, sendI, sendR,
    sums, recvS,
    s1_sem, r1_sem, s2_sem, r2_sem,
    hi_send, hi_recv, hr_send, hr_recv, own_sem, rs_send, rs_recv,
):
    me = lax.axis_index("ctx")
    hd = lax.axis_index("head")
    rows_out = TOKENS // heads

    barrier = pltpu.get_barrier_semaphore()
    for d in range(1, CTX):
        pl.semaphore_signal(barrier, inc=1, device_id={"ctx": lax.rem(me + d, CTX)}, device_id_type=MESH)
    for d in range(1, heads):
        pl.semaphore_signal(barrier, inc=1, device_id={"head": lax.rem(hd + d, heads)}, device_id_type=MESH)

    row = lax.broadcasted_iota(jnp.int32, (TOKENS, TOKENS), 0)
    col = lax.broadcasted_iota(jnp.int32, (TOKENS, TOKENS), 1)
    perm = jnp.where(col == (row % SEG) * LEN + row // SEG, 1.0, 0.0).astype(BF16)
    kp = jnp.dot(perm, k_ref[0], preferred_element_type=F32).astype(BF16)
    qp = jnp.dot(perm, q_ref[0], preferred_element_type=F32).astype(BF16)
    state_row = lax.broadcasted_iota(jnp.int32, (N, LANES), 0)
    norm = jnp.zeros((TOKENS, LANES), F32)
    for n in range(N):
        pick = jnp.where(state_row == n, 1.0, 0.0).astype(BF16)
        kn = jnp.dot(kp, pick, preferred_element_type=F32)
        qn = jnp.dot(qp, pick, preferred_element_type=F32)
        k2 = kn * kn
        norm = norm + k2
        for i in range(LEN):
            kT[i * N + n] = kn[i * SEG:(i + 1) * SEG]
            k2T[i * N + n] = k2[i * SEG:(i + 1) * SEG]
            qT[i * N + n] = qn[i * SEG:(i + 1) * SEG]
    for i in range(LEN):
        knT[i] = norm[i * SEG:(i + 1) * SEG]

    def first_pass(it, _):
        p = lax.rem(me // 4 + (PAIRS - 1 - it), PAIRS)
        lane0 = pl.multiple_of(p * WIDE, WIDE)
        for c in range(2):
            lanes = pl.ds(pl.multiple_of(lane0 + c * LANES, LANES), LANES)
            x32[c] = x_ref[0, :, lanes].astype(F32)
            g32[c] = g_ref[0, :, lanes].astype(F32)
            r32[c] = rate_ref[0, :, lanes]
        base = p * (2 * LEN)
        for i in range(LEN):
            for c in range(2):
                at = base + 2 * i + c
                rate = r32[c, pl.ds(i, SEG, stride=LEN), :]
                xv = x32[c, pl.ds(i, SEG, stride=LEN), :]
                gv = g32[c, pl.ds(i, SEG, stride=LEN), :]
                inv = 1.0 / (1.0 + rate * knT[i])
                step = rate * inv
                stepP[at] = step
                invP[at] = inv
                uP[at] = step * xv
                xP[at] = xv
                gP[at] = gv

        def n_group(ng, _):
            n0 = ng * 4
            prod = [None] * 8
            end = [None] * 8
            back = [None] * 8
            for i in range(LEN):
                step = [stepP[base + 2 * i + c] for c in range(2)]
                u = [uP[base + 2 * i + c] for c in range(2)]
                gv = [gP[base + 2 * i + c] for c in range(2)]
                for a in range(4):
                    kk = kT[i * N + n0 + a]
                    k2 = k2T[i * N + n0 + a]
                    qq = qT[i * N + n0 + a]
                    for c in range(2):
                        j = 2 * a + c
                        dec = 1.0 - step[c] * k2
                        emit = gv[c] * qq
                        drive = u[c] * kk
                        if i == 0:
                            prod[j] = dec
                            end[j] = drive
                            back[j] = emit * dec
                        else:
                            prod[j] = prod[j] * dec
                            end[j] = end[j] * dec + drive
                            back[j] = back[j] + emit * prod[j]
            for a in range(4):
                for c in range(2):
                    at = pl.multiple_of((c * N + n0 + a) * SEG, SEG)
                    sumP[pl.ds(at, SEG), :] = prod[2 * a + c]
                    sumL[pl.ds(at, SEG), :] = end[2 * a + c]
                    sumB[pl.ds(at, SEG), :] = back[2 * a + c]
            return 0

        lax.fori_loop(0, N // 4, n_group, 0)

        for j in range(4):
            o = p * 4 + j
            tile = j * 8 * SEG
            run_p = jnp.ones((SEG, LANES), F32)
            run_l = jnp.zeros((SEG, LANES), F32)
            ps, bs = [], []
            for s in range(SEG):
                pv = sumP[pl.ds(tile + s, SEG, stride=SEG), :]
                lv = sumL[pl.ds(tile + s, SEG, stride=SEG), :]
                ps.append(pv)
                bs.append(sumB[pl.ds(tile + s, SEG, stride=SEG), :])
                preP[o * SEG + s] = run_p
                preL[o * SEG + s] = run_l
                run_l = run_l * pv + lv
                run_p = run_p * pv
            send1[o, 0] = run_p
            send1[o, 1] = run_l
            run_p = jnp.ones((SEG, LANES), F32)
            run_b = jnp.zeros((SEG, LANES), F32)
            for s in reversed(range(SEG)):
                postP[o * SEG + s] = run_p
                postB[o * SEG + s] = run_b
                run_b = run_b * ps[s] + bs[s]
                run_p = run_p * ps[s]
            send1[o, 2] = run_b

        @pl.when(it == 0)
        def _():
            pl.semaphore_wait(barrier, CTX - 1 + heads - 1)

        for j in range(4):
            o = p * 4 + j

            @pl.when(o != me)
            def _():
                to_owner(o).start()

            @pl.when(o == me)
            def _():
                recv1[o] = send1[o]
        return 0

    def to_owner(o):
        return pltpu.make_async_remote_copy(
            src_ref=send1.at[o], dst_ref=recv1.at[me], send_sem=s1_sem.at[o], recv_sem=r1_sem.at[me],
            device_id={"ctx": o}, device_id_type=MESH)

    def from_group(o):
        return pltpu.make_async_remote_copy(
            src_ref=send1.at[o], dst_ref=recv1.at[o], send_sem=s1_sem.at[o], recv_sem=r1_sem.at[o],
            device_id={"ctx": o}, device_id_type=MESH)

    def to_group(o):
        return pltpu.make_async_remote_copy(
            src_ref=send2.at[o], dst_ref=recv2.at[me], send_sem=s2_sem.at[o], recv_sem=r2_sem.at[me],
            device_id={"ctx": o}, device_id_type=MESH)

    def from_owner(o):
        return pltpu.make_async_remote_copy(
            src_ref=send2.at[o], dst_ref=recv2.at[o], send_sem=s2_sem.at[o], recv_sem=r2_sem.at[o],
            device_id={"ctx": o}, device_id_type=MESH)

    lax.fori_loop(0, PAIRS, first_pass, 0)

    zero = jnp.zeros((SEG, LANES), F32)

    def clear(i, _):
        for n in range(N):
            accQ[i * N + n] = zero
            accK[i * N + n] = zero
        accN[i] = zero
        return 0

    lax.fori_loop(0, LEN, clear, 0)

    for d in range(1, CTX):
        from_group(lax.rem(me + d, CTX)).wait_recv()
    state = zero
    grad = zero
    for c in range(CTX):
        send2[c, 0] = state
        state = state * recv1[c, 0] + recv1[c, 1]
    for c in reversed(range(CTX)):
        send2[c, 1] = grad
        grad = grad * recv1[c, 0] + recv1[c, 2]
    for d in range(1, CTX):
        to_group(lax.rem(me + d, CTX)).start()
    recv2[me] = send2[me]

    def head_copy(array, p, h, src_buf, dst, ssem, rsem):
        return pltpu.make_async_remote_copy(
            src_ref=src_buf.at[p, pl.ds(pl.multiple_of(h * rows_out, rows_out), rows_out), :],
            dst_ref=dst.at[0, :, pl.ds(pl.multiple_of(array * (PAIRS * WIDE) + p * WIDE, WIDE), WIDE)],
            send_sem=ssem.at[p, h], recv_sem=rsem.at[p, array],
            device_id={"head": h}, device_id_type=MESH)

    def own_copy(p, which, src_buf, dst):
        return pltpu.make_async_copy(
            src_buf.at[p, pl.ds(pl.multiple_of(hd * rows_out, rows_out), rows_out), :],
            dst.at[0, :, pl.ds(pl.multiple_of(hd * (PAIRS * WIDE) + p * WIDE, WIDE), WIDE)],
            own_sem.at[p, which])

    def second_pass(it, _):
        p = lax.rem(me // 4 + it, PAIRS)
        base = p * (2 * LEN)
        for j in range(4):
            o = p * 4 + j

            @pl.when(o != me)
            def _():
                from_owner(o).wait_recv()

            s0 = recv2[o, 0]
            g0 = recv2[o, 1]
            tile = j * 8 * SEG
            for s in range(SEG):
                at = o * SEG + s
                sIn[pl.ds(tile + s, SEG, stride=SEG), :] = preP[at] * s0 + preL[at]
                gIn[pl.ds(tile + s, SEG, stride=SEG), :] = postP[at] * g0 + postB[at]

        def forward(i, states):
            states = list(states)
            step = [stepP[base + 2 * i + c] for c in range(2)]
            u = [uP[base + 2 * i + c] for c in range(2)]
            gv = [gP[base + 2 * i + c] for c in range(2)]
            for n in range(N):
                kk = kT[i * N + n]
                total = accQ[i * N + n]
                for c in range(2):
                    j = n * 2 + c
                    kprev = kk * states[j]
                    kpS[i * (2 * N) + j] = kprev
                    new = states[j] + kk * (u[c] - step[c] * kprev)
                    states[j] = new
                    total = total + gv[c] * new
                accQ[i * N + n] = total
            return tuple(states)

        start = tuple(sIn[pl.ds((c * N + n) * SEG, SEG), :] for n in range(N) for c in range(2))
        lax.fori_loop(0, LEN, forward, start)

        def backward(it2, grads):
            i = LEN - 1 - it2
            grads = list(grads)
            step = [stepP[base + 2 * i + c] for c in range(2)]
            twice = [s + s for s in step]
            u = [uP[base + 2 * i + c] for c in range(2)]
            gv = [gP[base + 2 * i + c] for c in range(2)]
            key_dot = [None, None]
            weighted = [None, None]
            for n in range(N):
                kk = kT[i * N + n]
                qq = qT[i * N + n]
                total = accK[i * N + n]
                for c in range(2):
                    j = n * 2 + c
                    kprev = kpS[i * (2 * N) + j]
                    grad = grads[j] + gv[c] * qq
                    gk = grad * kk
                    wk = gk * kprev
                    key_dot[c] = gk if n == 0 else key_dot[c] + gk
                    weighted[c] = wk if n == 0 else weighted[c] + wk
                    total = total + grad * (u[c] - twice[c] * kprev)
                    grads[j] = grad - kk * (step[c] * gk)
                accK[i * N + n] = total
            norm_sum = accN[i]
            for c in range(2):
                at = base + 2 * i + c
                inv = invP[at]
                outI[c, pl.ds(i, SEG, stride=LEN), :] = step[c] * key_dot[c]
                grad_step = xP[at] * key_dot[c] - weighted[c]
                outR[c, pl.ds(i, SEG, stride=LEN), :] = grad_step * (inv * inv)
                norm_sum = norm_sum + grad_step * (step[c] * step[c])
            accN[i] = norm_sum
            return tuple(grads)

        start = tuple(gIn[pl.ds((c * N + n) * SEG, SEG), :] for n in range(N) for c in range(2))
        lax.fori_loop(0, LEN, backward, start)
        for c in range(2):
            lanes = pl.ds(c * LANES, LANES)
            sendI[p, :, lanes] = outI[c].astype(BF16)
            sendR[p, :, lanes] = outR[c].astype(BF16)
        for d in range(1, heads):
            h = lax.rem(hd + d, heads)
            pltpu.make_async_remote_copy(
                src_ref=sendI.at[p, pl.ds(pl.multiple_of(h * rows_out, rows_out), rows_out), :],
                dst_ref=oi_ref.at[0, :, pl.ds(pl.multiple_of(hd * (PAIRS * WIDE) + p * WIDE, WIDE), WIDE)],
                send_sem=hi_send.at[p, h], recv_sem=hi_recv.at[p, hd],
                device_id={"head": h}, device_id_type=MESH).start()
            pltpu.make_async_remote_copy(
                src_ref=sendR.at[p, pl.ds(pl.multiple_of(h * rows_out, rows_out), rows_out), :],
                dst_ref=or_ref.at[0, :, pl.ds(pl.multiple_of(hd * (PAIRS * WIDE) + p * WIDE, WIDE), WIDE)],
                send_sem=hr_send.at[p, h], recv_sem=hr_recv.at[p, hd],
                device_id={"head": h}, device_id_type=MESH).start()
        own_copy(p, 0, sendI, oi_ref).start()
        own_copy(p, 1, sendR, or_ref).start()
        return 0

    lax.fori_loop(0, PAIRS, second_pass, 0)

    lane = lax.broadcasted_iota(jnp.int32, (SEG, LANES), 1)

    def reduce_lanes(i, _):
        merged = zero
        norm2 = accN[i] + accN[i]
        for n in range(N):
            key = accK[i * N + n] - kT[i * N + n] * norm2
            merged = jnp.where(lane == n, jnp.sum(key, axis=1, keepdims=True), merged)
            merged = jnp.where(lane == N + n, jnp.sum(accQ[i * N + n], axis=1, keepdims=True), merged)
        sums[pl.ds(i, SEG, stride=LEN), :] = merged
        return 0

    lax.fori_loop(0, LEN, reduce_lanes, 0)

    def sum_copy(h, src):
        return pltpu.make_async_remote_copy(
            src_ref=sums.at[pl.ds(pl.multiple_of(h * rows_out, rows_out), rows_out), :],
            dst_ref=recvS.at[src], send_sem=rs_send.at[h], recv_sem=rs_recv.at[src],
            device_id={"head": h}, device_id_type=MESH)

    for d in range(1, heads):
        sum_copy(lax.rem(hd + d, heads), hd).start()
    recvS[hd] = sums[pl.ds(pl.multiple_of(hd * rows_out, rows_out), rows_out), :]

    for d in range(1, CTX):
        o = lax.rem(me + d, CTX)
        to_owner(o).wait_send()
        to_group(o).wait_send()
    for p in range(PAIRS):
        own_copy(p, 0, sendI, oi_ref).wait()
        own_copy(p, 1, sendR, or_ref).wait()
        for d in range(1, heads):
            h = lax.rem(hd + d, heads)
            for buf, dst, ssem, rsem in ((sendI, oi_ref, hi_send, hi_recv), (sendR, or_ref, hr_send, hr_recv)):
                copy = head_copy(h, p, h, buf, dst, ssem, rsem)
                copy.wait_send()
                copy.wait_recv()
    for d in range(1, heads):
        h = lax.rem(hd + d, heads)
        copy = sum_copy(h, h)
        copy.wait_send()
        copy.wait_recv()
    total = recvS[0]
    for h in range(1, heads):
        total = total + recvS[h]
    ok_ref[0] = total[:, :N]
    oq_ref[0] = total[:, N:2 * N]


def shards(heads):
    def run(inputs, step_rate, key_rows, query_rows, grad_out):
        rows_out = TOKENS // heads
        width = heads * PAIRS * WIDE
        vmem = pl.BlockSpec(memory_space=pltpu.VMEM)
        hbm = pl.BlockSpec(memory_space=pl.ANY)
        tile = (SEG, LANES)

        def regs(*lead):
            return pltpu.VMEM(lead + tile, F32)

        dma = pltpu.SemaphoreType.DMA
        return pl.pallas_call(
            lambda *refs: kernel(heads, *refs),
            out_shape=(
                jax.ShapeDtypeStruct((1, rows_out, width), BF16),
                jax.ShapeDtypeStruct((1, rows_out, width), BF16),
                jax.ShapeDtypeStruct((1, rows_out, N), F32),
                jax.ShapeDtypeStruct((1, rows_out, N), F32),
            ),
            in_specs=[vmem] * 5,
            out_specs=(hbm, hbm, vmem, vmem),
            scratch_shapes=[
                regs(LEN * N), regs(LEN * N), regs(LEN * N), regs(LEN),
                *[pltpu.VMEM((2, TOKENS, LANES), F32) for _ in range(3)],
                *[regs(PAIRS * 2 * LEN) for _ in range(5)],
                *[pltpu.VMEM((2 * N * SEG, LANES), F32) for _ in range(3)],
                *[regs(CTX * SEG) for _ in range(4)],
                regs(CTX, 3), regs(CTX, 3), regs(CTX, 2), regs(CTX, 2),
                pltpu.VMEM((2 * N * SEG, LANES), F32), pltpu.VMEM((2 * N * SEG, LANES), F32),
                regs(LEN * 2 * N),
                regs(LEN * N), regs(LEN * N), regs(LEN),
                pltpu.VMEM((2, TOKENS, LANES), F32), pltpu.VMEM((2, TOKENS, LANES), F32),
                pltpu.VMEM((PAIRS, TOKENS, WIDE), BF16), pltpu.VMEM((PAIRS, TOKENS, WIDE), BF16),
                pltpu.VMEM((TOKENS, LANES), F32), pltpu.VMEM((heads, rows_out, LANES), F32),
                dma((CTX,)), dma((CTX,)), dma((CTX,)), dma((CTX,)),
                dma((PAIRS, heads)), dma((PAIRS, heads)), dma((PAIRS, heads)), dma((PAIRS, heads)),
                dma((PAIRS, 2)), dma((heads,)), dma((heads,)),
            ],
            compiler_params=pltpu.CompilerParams(
                collective_id=0, has_side_effects=True, vmem_limit_bytes=48 * 1024 * 1024),
        )(inputs, step_rate, key_rows, query_rows, grad_out)

    return run


def solution(mesh):
    placed = (
        P("dp", "ctx", "head"),
        P("dp", "ctx", "head"),
        P("dp", "ctx", None),
        P("dp", "ctx", None),
        P("dp", "ctx", "head"),
    )
    out = P("dp", ("ctx", "head"), None)
    return jax.shard_map(
        shards(mesh.shape["head"]),
        mesh=mesh,
        in_specs=placed,
        out_specs=(out, out, out, out),
        check_vma=False,
    )
```

profile of v0, /device:TPU:6, one launch (start us, length us, event | category | flops | bytes accessed | tf_op | source)
XLA Modules:
  0.0 42.0 jit_solution(14716678624329437488)
XLA Ops:
  0.6 0.0 copy-start.3
  0.6 0.8 %copy.9.refs_2_ = bf16[1,128,16]{2,1,0:T(8,128)(2,1)S(1)} copy(bf16[1,128,16]{1,2,0:T(8,128)(2,1)} %param.7) | data formatting | bytes 8192 | tf_op args[2]
  1.4 0.0 copy-done.3
  1.5 0.1 copy.10.refs_3_
  1.6 0.0 copy-start
  1.6 1.0 %copy-done = f32[1,128,1024]{2,1,0:T(8,128)S(1)} copy-done((f32[1,128,1024]{2,1,0:T(8,128)S(1)}, f32[1,128,1024]{2,1,0:T(8,128)}, u32[]{:S(2)}) %copy-start) | copy-done | bytes 524312
  2.6 0.0 copy-start.1
  2.6 0.9 %copy-done.1 = bf16[1,128,1024]{2,1,0:T(8,128)(2,1)S(1)} copy-done((bf16[1,128,1024]{2,1,0:T(8,128)(2,1)S(1)}, bf16[1,128,1024]{2,1,0:T(8,128)(2,1)}, u32[]{:S(2)}) %copy-start.1) | copy-done | bytes 262168
  3.6 0.0 copy-start.2
  3.6 0.9 %copy-done.2 = bf16[1,128,1024]{2,1,0:T(8,128)(2,1)S(1)} copy-done((bf16[1,128,1024]{2,1,0:T(8,128)(2,1)S(1)}, bf16[1,128,1024]{2,1,0:T(8,128)(2,1)}, u32[]{:S(2)}) %copy-start.2) | copy-done | bytes 262168
  4.5 34.7 %shard_map.84 = (bf16[1,32,4096]{2,1,0:T(8,128)(2,1)S(1)}, bf16[1,32,4096]{2,1,0:T(8,128)(2,1)S(1)}, f32[1,32,16]{2,1,0:T(8,128)S(1)}, f32[1,32,16]{2,1,0:T(8,128)S(1)}) custom-call(bf16[1,128,1024]{2,1,0:T(8,128)(2,1)S(1)} %copy-done.1, f32[1,128,1024]{2,1,0:T(8,128)S(1)} %copy-done, bf16[1,128,16]{2,1,0:T(8,128)(2,1)S(1)} %copy.9.refs_2_, ...), custom_call_target="tpu_custom_call" | custom-call | tf_op jit(solution)/shard_map/pallas_call | solution.py:389
  39.2 0.7 %copy.11 = f32[1,32,16]{1,2,0:T(8,128)} copy(f32[1,32,16]{2,1,0:T(8,128)S(1)} %get-tuple-element.6) | data formatting | bytes 4096 | tf_op jit(solution)/shard_map/pallas_call | solution.py:389
  39.9 0.7 %copy.12 = f32[1,32,16]{1,2,0:T(8,128)} copy(f32[1,32,16]{2,1,0:T(8,128)S(1)} %get-tuple-element.7) | data formatting | bytes 4096 | tf_op jit(solution)/shard_map/pallas_call | solution.py:389
  40.6 0.7 %copy.15 = bf16[1,32,4096]{2,1,0:T(8,128)(2,1)} copy(bf16[1,32,4096]{2,1,0:T(8,128)(2,1)S(1)} %get-tuple-element.12) | data formatting | bytes 524288
  41.3 0.7 %copy.16 = bf16[1,32,4096]{2,1,0:T(8,128)(2,1)} copy(bf16[1,32,4096]{2,1,0:T(8,128)(2,1)S(1)} %get-tuple-element.13) | data formatting | bytes 524288
Async XLA Ops:
  0.6 0.8 %copy-start.3 = (bf16[1,128,16]{1,2,0:T(8,128)(2,1)S(1)}, bf16[1,128,16]{1,2,0:T(8,128)(2,1)}, u32[]{:S(2)}) copy-start(bf16[1,128,16]{1,2,0:T(8,128)(2,1)} %param.8) | copy-start | bytes 12292
  1.6 1.0 %copy-start = (f32[1,128,1024]{2,1,0:T(8,128)S(1)}, f32[1,128,1024]{2,1,0:T(8,128)}, u32[]{:S(2)}) copy-start(f32[1,128,1024]{2,1,0:T(8,128)} %refs_1_.1) | copy-start | bytes 1572868
  2.6 0.9 %copy-start.1 = (bf16[1,128,1024]{2,1,0:T(8,128)(2,1)S(1)}, bf16[1,128,1024]{2,1,0:T(8,128)(2,1)}, u32[]{:S(2)}) copy-start(bf16[1,128,1024]{2,1,0:T(8,128)(2,1)} %refs_0_.1) | copy-start | bytes 786436
  3.6 0.9 %copy-start.2 = (bf16[1,128,1024]{2,1,0:T(8,128)(2,1)S(1)}, bf16[1,128,1024]{2,1,0:T(8,128)(2,1)}, u32[]{:S(2)}) copy-start(bf16[1,128,1024]{2,1,0:T(8,128)(2,1)} %refs_4_.1) | copy-start | bytes 786436
where the time goes:
time: 42.5 us; the launch traced here: 42 us
  Pallas kernels  34.7 us (82%)
  local copies, waits for them, and re-layouts  6.62 us (16%)
  between operations  0.66 us (2%)
    pallas_call x1, Pallas kernels, run(): pl.pallas_call(lambda *refs: kernel(heads, *refs), out_shape=(jax.ShapeDt...  34.7 us
    unnamed x12, local copies, waits for them, and re-layouts  5.28 us
    pallas_call x2, local copies, waits for them, and re-layouts, run(): pl.pallas_call(lambda *refs: kernel(heads, *refs), out_shape=(jax.ShapeDt...  1.34 us

commit v1 on v0

v1 whole, which is shorter than its diff:
```python
import jax
import jax.numpy as jnp
from jax import lax
from jax.experimental import pallas as pl
from jax.experimental.pallas import tpu as pltpu
from jax.sharding import PartitionSpec as P

MESH = pl.DeviceIdType.MESH
F32 = jnp.float32
BF16 = jnp.bfloat16

SEG = 8
LEN = 16
N = 16
LANES = 128
PAIRS = 4
WIDE = 256
CTX = 16
STEPS = 2
TOKENS = SEG * LEN


def owner_of(p, j):
    return 2 * (2 * j + p % 2) + p // 2


def kernel(
    heads,
    x_ref, rate_ref, k_ref, q_ref, g_ref,
    oi_ref, or_ref, rs_ref,
    xV, rV, gV, kV, qV,
    kT, k2T, qT, knT, kL,
    x32, g32, r32,
    stepP, uP, gP, xP, invP, decS,
    sumP, sumL, sumB,
    preP, preL, postP, postB,
    send1, recv1, send2, recv2,
    sIn, gIn, kpS,
    accQ, accK, accN,
    outI, outR, sendI, sendR,
    sums,
    in_sem, s1_sem, r1_sem, s2_sem, r2_sem,
    hi_send, hi_recv, hr_send, hr_recv, own_sem, rs_send, rs_recv,
):
    me = lax.axis_index("ctx")
    hd = lax.axis_index("head")
    rows_out = TOKENS // heads
    my_pair = 2 * lax.rem(me, 2) + lax.rem(me // 2, 2)
    my_tile = my_pair * 4 + me // 4

    k_copy = pltpu.make_async_copy(k_ref.at[0], kV, in_sem.at[3 * PAIRS])
    q_copy = pltpu.make_async_copy(q_ref.at[0], qV, in_sem.at[3 * PAIRS + 1])
    k_copy.start()
    q_copy.start()

    def in_copy(p, which):
        ref, buf = ((x_ref, xV), (rate_ref, rV), (g_ref, gV))[which]
        lanes = pl.ds(p * WIDE, WIDE) if isinstance(p, int) else pl.ds(pl.multiple_of(p * WIDE, WIDE), WIDE)
        return pltpu.make_async_copy(ref.at[0, :, lanes], buf.at[p], in_sem.at[p * 3 + which])

    for p in range(PAIRS):
        for which in range(3):
            in_copy(p, which).start()

    barrier = pltpu.get_barrier_semaphore()
    for d in range(1, CTX):
        pl.semaphore_signal(barrier, inc=1, device_id={"ctx": lax.rem(me + d, CTX)}, device_id_type=MESH)
    for d in range(1, heads):
        pl.semaphore_signal(barrier, inc=1, device_id={"head": lax.rem(hd + d, heads)}, device_id_type=MESH)

    row = lax.broadcasted_iota(jnp.int32, (TOKENS, TOKENS), 0)
    col = lax.broadcasted_iota(jnp.int32, (TOKENS, TOKENS), 1)
    perm = jnp.where(col == (row % SEG) * LEN + row // SEG, 1.0, 0.0).astype(BF16)
    state_row = lax.broadcasted_iota(jnp.int32, (N, LANES), 0)
    state_col = lax.broadcasted_iota(jnp.int32, (N, LANES), 1)
    k_copy.wait()
    q_copy.wait()
    last = (((1,), (1,)), ((), ()))
    kp = lax.dot_general(perm, kV[...], last, preferred_element_type=F32).astype(BF16)
    qp = lax.dot_general(perm, qV[...], last, preferred_element_type=F32).astype(BF16)
    kL[...] = jnp.dot(kp, jnp.where(state_row == state_col, 1.0, 0.0).astype(BF16), preferred_element_type=F32)
    norm = jnp.zeros((TOKENS, LANES), F32)
    for n in range(N):
        pick = jnp.where(state_row == n, 1.0, 0.0).astype(BF16)
        kn = jnp.dot(kp, pick, preferred_element_type=F32)
        qn = jnp.dot(qp, pick, preferred_element_type=F32)
        k2 = kn * kn
        norm = norm + k2
        for i in range(LEN):
            kT[i * N + n] = kn[i * SEG:(i + 1) * SEG]
            k2T[i * N + n] = k2[i * SEG:(i + 1) * SEG]
            qT[i * N + n] = qn[i * SEG:(i + 1) * SEG]
    for i in range(LEN):
        knT[i] = norm[i * SEG:(i + 1) * SEG]

    def to_owner(p, j):
        o = owner_of(p, j)
        return pltpu.make_async_remote_copy(
            src_ref=send1.at[p * 4 + j], dst_ref=recv1.at[me], send_sem=s1_sem.at[p * 4 + j],
            recv_sem=r1_sem.at[me], device_id={"ctx": o}, device_id_type=MESH)

    def from_group(o):
        return pltpu.make_async_remote_copy(
            src_ref=send1.at[0], dst_ref=recv1.at[o], send_sem=s1_sem.at[0], recv_sem=r1_sem.at[o],
            device_id={"ctx": o}, device_id_type=MESH)

    def to_group(o):
        return pltpu.make_async_remote_copy(
            src_ref=send2.at[o], dst_ref=recv2.at[my_tile], send_sem=s2_sem.at[o], recv_sem=r2_sem.at[my_tile],
            device_id={"ctx": o}, device_id_type=MESH)

    def from_owner(p, j):
        return pltpu.make_async_remote_copy(
            src_ref=send2.at[0], dst_ref=recv2.at[p * 4 + j], send_sem=s2_sem.at[0],
            recv_sem=r2_sem.at[p * 4 + j], device_id={"ctx": owner_of(p, j)}, device_id_type=MESH)

    def own_scan():
        for d in range(1, CTX):
            from_group(lax.rem(me + d, CTX)).wait_recv()
        state = jnp.zeros((SEG, LANES), F32)
        grad = state
        for c in range(CTX):
            send2[c, 0] = state
            state = state * recv1[c, 0] + recv1[c, 1]
        for c in reversed(range(CTX)):
            send2[c, 1] = grad
            grad = grad * recv1[c, 0] + recv1[c, 2]
        for d in range(1, CTX):
            to_group(lax.rem(me + d, CTX)).start()
        recv2[my_tile] = send2[me]

    def first_pass(p, _):
        for which in range(3):
            in_copy(p, which).wait()
        for c in range(2):
            lanes = pl.ds(c * LANES, LANES)
            x32[c] = xV[p, :, lanes].astype(F32)
            g32[c] = gV[p, :, lanes].astype(F32)
            r32[c] = rV[p, :, lanes]
        base = p * (2 * LEN)
        for i in range(LEN):
            for c in range(2):
                at = base + 2 * i + c
                rate = r32[c, pl.ds(i, SEG, stride=LEN), :]
                xv = x32[c, pl.ds(i, SEG, stride=LEN), :]
                gv = g32[c, pl.ds(i, SEG, stride=LEN), :]
                inv = 1.0 / (1.0 + rate * knT[i])
                step = rate * inv
                stepP[at] = step
                invP[at] = inv
                uP[at] = step * xv
                xP[at] = xv
                gP[at] = gv

        def n_group(ng, _):
            n0 = ng * 4
            prod = [None] * 8
            end = [None] * 8
            back = [None] * 8
            for i in range(LEN):
                step = [stepP[base + 2 * i + c] for c in range(2)]
                u = [uP[base + 2 * i + c] for c in range(2)]
                gv = [gP[base + 2 * i + c] for c in range(2)]
                for a in range(4):
                    kk = kT[i * N + n0 + a]
                    k2 = k2T[i * N + n0 + a]
                    qq = qT[i * N + n0 + a]
                    for c in range(2):
                        j = 2 * a + c
                        dec = 1.0 - step[c] * k2
                        decS[(p * LEN + i) * (2 * N) + 2 * n0 + j] = dec
                        emit = gv[c] * qq
                        drive = u[c] * kk
                        if i == 0:
                            prod[j] = dec
                            end[j] = drive
                            back[j] = emit * dec
                        else:
                            prod[j] = prod[j] * dec
                            end[j] = end[j] * dec + drive
                            back[j] = back[j] + emit * prod[j]
            for a in range(4):
                for c in range(2):
                    at = pl.multiple_of((c * N + n0 + a) * SEG, SEG)
                    sumP[pl.ds(at, SEG), :] = prod[2 * a + c]
                    sumL[pl.ds(at, SEG), :] = end[2 * a + c]
                    sumB[pl.ds(at, SEG), :] = back[2 * a + c]
            return 0

        lax.fori_loop(0, N // 4, n_group, 0)

        for j in range(4):
            o = p * 4 + j
            tile = j * 8 * SEG
            run_p = jnp.ones((SEG, LANES), F32)
            run_l = jnp.zeros((SEG, LANES), F32)
            ps, bs = [], []
            for s in range(SEG):
                pv = sumP[pl.ds(tile + s, SEG, stride=SEG), :]
                lv = sumL[pl.ds(tile + s, SEG, stride=SEG), :]
                ps.append(pv)
                bs.append(sumB[pl.ds(tile + s, SEG, stride=SEG), :])
                preP[o * SEG + s] = run_p
                preL[o * SEG + s] = run_l
                run_l = run_l * pv + lv
                run_p = run_p * pv
            send1[o, 0] = run_p
            send1[o, 1] = run_l
            run_p = jnp.ones((SEG, LANES), F32)
            run_b = jnp.zeros((SEG, LANES), F32)
            for s in reversed(range(SEG)):
                postP[o * SEG + s] = run_p
                postB[o * SEG + s] = run_b
                run_b = run_b * ps[s] + bs[s]
                run_p = run_p * ps[s]
            send1[o, 2] = run_b

        @pl.when(p == 0)
        def _():
            pl.semaphore_wait(barrier, CTX - 1 + heads - 1)

        for j in range(4):
            @pl.when(owner_of(p, j) != me)
            def _():
                to_owner(p, j).start()

            @pl.when(owner_of(p, j) == me)
            def _():
                recv1[me] = send1[p * 4 + j]

        @pl.when((p >= 2) & (my_pair == p - 2))
        def _():
            own_scan()
        return 0

    lax.fori_loop(0, PAIRS, first_pass, 0)

    zero = jnp.zeros((SEG, LANES), F32)

    def clear(i, _):
        for n in range(N):
            accQ[i * N + n] = zero
            accK[i * N + n] = zero
        accN[i] = zero
        return 0

    lax.fori_loop(0, LEN, clear, 0)

    @pl.when(my_pair == 2)
    def _():
        own_scan()

    def head_copy(p, h, owner, src_buf, dst, ssem, rsem):
        return pltpu.make_async_remote_copy(
            src_ref=src_buf.at[p, pl.ds(pl.multiple_of(h * rows_out, rows_out), rows_out), :],
            dst_ref=dst.at[0, :, pl.ds(pl.multiple_of(owner * (PAIRS * WIDE) + p * WIDE, WIDE), WIDE)],
            send_sem=ssem.at[p, h], recv_sem=rsem.at[p, owner],
            device_id={"head": h}, device_id_type=MESH)

    def own_copy(p, which, src_buf, dst):
        return pltpu.make_async_copy(
            src_buf.at[p, pl.ds(pl.multiple_of(hd * rows_out, rows_out), rows_out), :],
            dst.at[0, :, pl.ds(pl.multiple_of(hd * (PAIRS * WIDE) + p * WIDE, WIDE), WIDE)],
            own_sem.at[p, which])

    arrays = ((sendI, oi_ref, hi_send, hi_recv), (sendR, or_ref, hr_send, hr_recv))

    def second_pass(p, _):
        base = p * (2 * LEN)
        for j in range(4):
            o = p * 4 + j

            @pl.when(owner_of(p, j) != me)
            def _():
                from_owner(p, j).wait_recv()

            s0 = recv2[o, 0]
            g0 = recv2[o, 1]
            tile = j * 8 * SEG
            for s in range(SEG):
                at = o * SEG + s
                sIn[pl.ds(tile + s, SEG, stride=SEG), :] = preP[at] * s0 + preL[at]
                gIn[pl.ds(tile + s, SEG, stride=SEG), :] = postP[at] * g0 + postB[at]

        def forward(i, states):
            states = list(states)
            u = [uP[base + 2 * i + c] for c in range(2)]
            gv = [gP[base + 2 * i + c] for c in range(2)]
            for n in range(N):
                kk = kT[i * N + n]
                total = accQ[i * N + n]
                for c in range(2):
                    j = n * 2 + c
                    kpS[i * (2 * N) + j] = kk * states[j]
                    states[j] = decS[(p * LEN + i) * (2 * N) + j] * states[j] + u[c] * kk
                    total = total + gv[c] * states[j]
                accQ[i * N + n] = total
            return tuple(states)

        start = tuple(sIn[pl.ds((c * N + n) * SEG, SEG), :] for n in range(N) for c in range(2))
        def forward_some(b, states):
            for r in range(STEPS):
                states = forward(b * STEPS + r, states)
            return states

        lax.fori_loop(0, LEN // STEPS, forward_some, start)

        def backward(it2, grads):
            i = LEN - 1 - it2
            grads = list(grads)
            step = [stepP[base + 2 * i + c] for c in range(2)]
            twice = [s + s for s in step]
            u = [uP[base + 2 * i + c] for c in range(2)]
            gv = [gP[base + 2 * i + c] for c in range(2)]
            key_dot = [None, None]
            weighted = [None, None]
            for n in range(N):
                kk = kT[i * N + n]
                qq = qT[i * N + n]
                total = accK[i * N + n]
                for c in range(2):
                    j = n * 2 + c
                    kprev = kpS[i * (2 * N) + j]
                    grad = grads[j] + gv[c] * qq
                    gk = grad * kk
                    wk = gk * kprev
                    key_dot[c] = gk if n == 0 else key_dot[c] + gk
                    weighted[c] = wk if n == 0 else weighted[c] + wk
                    total = total + grad * (u[c] - twice[c] * kprev)
                    grads[j] = grad * decS[(p * LEN + i) * (2 * N) + j]
                accK[i * N + n] = total
            norm_sum = accN[i]
            for c in range(2):
                at = base + 2 * i + c
                inv = invP[at]
                outI[c, pl.ds(i, SEG, stride=LEN), :] = step[c] * key_dot[c]
                grad_step = xP[at] * key_dot[c] - weighted[c]
                outR[c, pl.ds(i, SEG, stride=LEN), :] = grad_step * (inv * inv)
                norm_sum = norm_sum + grad_step * (step[c] * step[c])
            accN[i] = norm_sum
            return tuple(grads)

        start = tuple(gIn[pl.ds((c * N + n) * SEG, SEG), :] for n in range(N) for c in range(2))
        def backward_some(b, grads):
            for r in range(STEPS):
                grads = backward(b * STEPS + r, grads)
            return grads

        lax.fori_loop(0, LEN // STEPS, backward_some, start)
        for c in range(2):
            lanes = pl.ds(c * LANES, LANES)
            sendI[p, :, lanes] = outI[c].astype(BF16)
            sendR[p, :, lanes] = outR[c].astype(BF16)
        for d in range(1, heads):
            for src_buf, dst, ssem, rsem in arrays:
                head_copy(p, lax.rem(hd + d, heads), hd, src_buf, dst, ssem, rsem).start()
        own_copy(p, 0, sendI, oi_ref).start()
        own_copy(p, 1, sendR, or_ref).start()

        @pl.when((p == 0) & (my_pair == 3))
        def _():
            own_scan()
        return 0

    lax.fori_loop(0, PAIRS, second_pass, 0)

    ones = jnp.ones((2 * LANES, LANES), BF16)
    lane = lax.broadcasted_iota(jnp.int32, (TOKENS, LANES), 1)

    def lane_sums(parts):
        whole = jnp.concatenate(parts, axis=0)
        high = whole.astype(BF16)
        low = (whole - high.astype(F32)).astype(BF16)
        return jnp.dot(jnp.concatenate([high, low], axis=1), ones, preferred_element_type=F32)

    merged = lane_sums([accN[i] for i in range(LEN)]) * (-2.0 * kL[...])
    for n in range(N):
        merged = jnp.where(lane == n, merged + lane_sums([accK[i * N + n] for i in range(LEN)]), merged)
        merged = jnp.where(lane == N + n, lane_sums([accQ[i * N + n] for i in range(LEN)]), merged)
    for i in range(LEN):
        sums[pl.ds(i, SEG, stride=LEN), :] = merged[i * SEG:(i + 1) * SEG]

    def sum_copy(h, src):
        return pltpu.make_async_remote_copy(
            src_ref=sums.at[pl.ds(pl.multiple_of(h * rows_out, rows_out), rows_out), :], dst_ref=rs_ref.at[src], send_sem=rs_send.at[h], recv_sem=rs_recv.at[src],
            device_id={"head": h}, device_id_type=MESH)

    for d in range(1, heads):
        sum_copy(lax.rem(hd + d, heads), hd).start()
    rs_ref[hd] = sums[pl.ds(pl.multiple_of(hd * rows_out, rows_out), rows_out), :]

    for p in range(PAIRS):
        for j in range(4):
            @pl.when(owner_of(p, j) != me)
            def _():
                to_owner(p, j).wait_send()
    for d in range(1, CTX):
        to_group(lax.rem(me + d, CTX)).wait_send()
    for p in range(PAIRS):
        own_copy(p, 0, sendI, oi_ref).wait()
        own_copy(p, 1, sendR, or_ref).wait()
        for d in range(1, heads):
            h = lax.rem(hd + d, heads)
            for src_buf, dst, ssem, rsem in arrays:
                copy = head_copy(p, h, h, src_buf, dst, ssem, rsem)
                copy.wait_send()
                copy.wait_recv()
    for d in range(1, heads):
        h = lax.rem(hd + d, heads)
        copy = sum_copy(h, h)
        copy.wait_send()
        copy.wait_recv()


def finish(heads, i_ref, r_ref, s_ref, oi_ref, or_ref, ok_ref, oq_ref, small, sem):
    first = pltpu.make_async_copy(i_ref, oi_ref, sem.at[0])
    second = pltpu.make_async_copy(r_ref, or_ref, sem.at[1])
    first.start()
    second.start()
    total = s_ref[0]
    for h in range(1, heads):
        total = total + s_ref[h]
    turned = total.T
    small[0] = turned[:N]
    small[1] = turned[N:2 * N]
    third = pltpu.make_async_copy(small.at[0], ok_ref.at[0], sem.at[2])
    fourth = pltpu.make_async_copy(small.at[1], oq_ref.at[0], sem.at[3])
    third.start()
    fourth.start()
    for copy in (first, second, third, fourth):
        copy.wait()


def shards(heads):
    def run(inputs, step_rate, key_rows, query_rows, grad_out):
        rows_out = TOKENS // heads
        width = heads * PAIRS * WIDE
        vmem = pl.BlockSpec(memory_space=pltpu.VMEM)
        hbm = pl.BlockSpec(memory_space=pltpu.HBM)
        tile = (SEG, LANES)

        def regs(*lead):
            return pltpu.VMEM(lead + tile, F32)

        dma = pltpu.SemaphoreType.DMA
        wide = jax.ShapeDtypeStruct((1, rows_out, width), BF16)
        small = jax.ShapeDtypeStruct((1, N, rows_out), F32)
        grads_in, grads_rate, partial = pl.pallas_call(
            lambda *refs: kernel(heads, *refs),
            out_shape=(
                pltpu.VMEM((1, rows_out, width), BF16),
                pltpu.VMEM((1, rows_out, width), BF16),
                pltpu.VMEM((heads, rows_out, LANES), F32),
            ),
            in_specs=[hbm] * 5,
            out_specs=(vmem, vmem, vmem),
            scratch_shapes=[
                pltpu.VMEM((PAIRS, TOKENS, WIDE), BF16), pltpu.VMEM((PAIRS, TOKENS, WIDE), F32),
                pltpu.VMEM((PAIRS, TOKENS, WIDE), BF16),
                pltpu.VMEM((N, TOKENS), BF16), pltpu.VMEM((N, TOKENS), BF16),
                regs(LEN * N), regs(LEN * N), regs(LEN * N), regs(LEN), pltpu.VMEM((TOKENS, LANES), F32),
                *[pltpu.VMEM((2, TOKENS, LANES), F32) for _ in range(3)],
                *[regs(PAIRS * 2 * LEN) for _ in range(5)],
                regs(PAIRS * LEN * 2 * N),
                *[pltpu.VMEM((2 * N * SEG, LANES), F32) for _ in range(3)],
                *[regs(CTX * SEG) for _ in range(4)],
                regs(CTX, 3), regs(CTX, 3), regs(CTX, 2), regs(CTX, 2),
                pltpu.VMEM((2 * N * SEG, LANES), F32), pltpu.VMEM((2 * N * SEG, LANES), F32),
                regs(LEN * 2 * N),
                regs(LEN * N), regs(LEN * N), regs(LEN),
                pltpu.VMEM((2, TOKENS, LANES), F32), pltpu.VMEM((2, TOKENS, LANES), F32),
                pltpu.VMEM((PAIRS, TOKENS, WIDE), BF16), pltpu.VMEM((PAIRS, TOKENS, WIDE), BF16),
                pltpu.VMEM((TOKENS, LANES), F32),
                dma((3 * PAIRS + 2,)),
                dma((CTX,)), dma((CTX,)), dma((CTX,)), dma((CTX,)),
                dma((PAIRS, heads)), dma((PAIRS, heads)), dma((PAIRS, heads)), dma((PAIRS, heads)),
                dma((PAIRS, 2)), dma((heads,)), dma((heads,)),
            ],
            compiler_params=pltpu.CompilerParams(
                collective_id=0, has_side_effects=True, vmem_limit_bytes=48 * 1024 * 1024),
        )(*(
            pltpu.with_memory_space_constraint(a, pltpu.HBM)
            for a in (inputs, step_rate, jnp.swapaxes(key_rows, 1, 2), jnp.swapaxes(query_rows, 1, 2), grad_out)
        ))
        grads_in, grads_rate, keys, queries = pl.pallas_call(
            lambda *refs: finish(heads, *refs),
            out_shape=(wide, wide, small, small),
            in_specs=[vmem, vmem, vmem],
            out_specs=(hbm, hbm, hbm, hbm),
            scratch_shapes=[pltpu.VMEM((2, N, rows_out), F32), dma((4,))],
        )(*(pltpu.with_memory_space_constraint(a, pltpu.VMEM) for a in (grads_in, grads_rate, partial)))
        return grads_in, grads_rate, jnp.swapaxes(keys, 1, 2), jnp.swapaxes(queries, 1, 2)

    return run


def solution(mesh):
    placed = (
        P("dp", "ctx", "head"),
        P("dp", "ctx", "head"),
        P("dp", "ctx", None),
        P("dp", "ctx", None),
        P("dp", "ctx", "head"),
    )
    out = P("dp", ("ctx", "head"), None)
    return jax.shard_map(
        shards(mesh.shape["head"]),
        mesh=mesh,
        in_specs=placed,
        out_specs=(out, out, out, out),
        check_vma=False,
    )
```

time: 42.5 us -> 34.8 us (0.82)
  the two profiles are of different devices: /device:TPU:6 before, /device:TPU:1 now
where the time goes in v1:
time: 34.8 us; the launch traced here: 34.7 us
  Pallas kernels  34 us (98%)
  between operations  0.64 us (2%)
    pallas_call x1, Pallas kernels, run(): pl.pallas_call(lambda *refs: kernel(heads, *refs), out_shape=(pltpu.VMEM(...  33.2 us
    pallas_call x1, Pallas kernels, run(): pl.pallas_call(lambda *refs: finish(heads, *refs), out_shape=(wide, wide,...  0.83 us

profile of v1, /device:TPU:1, one launch (start us, length us, event | category | flops | bytes accessed | tf_op | source)
XLA Modules:
  0.0 34.7 jit_solution(17984005011723139219)
XLA Ops:
  0.6 33.2 %shard_map.84 = (bf16[1,32,4096]{2,1,0:T(8,128)(2,1)S(1)}, bf16[1,32,4096]{2,1,0:T(8,128)(2,1)S(1)}, f32[4,32,128]{2,1,0:T(8,128)S(1)}) custom-call(bf16[1,128,1024]{2,1,0:T(8,128)(2,1)} %refs_0_.1, f32[1,128,1024]{2,1,0:T(8,128)} %refs_1_.1, bf16[1,16,128]{2,1,0:T(8,128)(2,1)} %bitcast.4, bf16[1,16,128]{2,1,0:T(8,128)(2,1)} %bitcast.5, ...), custom_call_target="tpu_custom_call" | custom-call | tf_op jit(solution)/shard_map/pallas_call | solution.py:448
  33.9 0.8 %shard_map.85 = (bf16[1,32,4096]{2,1,0:T(8,128)(2,1)}, bf16[1,32,4096]{2,1,0:T(8,128)(2,1)}, f32[1,16,32]{2,1,0:T(8,128)}, f32[1,16,32]{2,1,0:T(8,128)}) custom-call(bf16[1,32,4096]{2,1,0:T(8,128)(2,1)S(1)} %get-tuple-element.11.refs_0_, bf16[1,32,4096]{2,1,0:T(8,128)(2,1)S(1)} %get-tuple-element.12.refs_1_, f32[4,32,128]{2,1,0:T(8,128)S(1)} %get-tuple-element.13.refs_2_), custom_call_target="tpu_custom_call" | custom-call | tf_op jit(solution)/shard_map/pallas_call | solution.py:485

commit v2 on v1

--- a/solution.py
+++ b/solution.py
@@ -16,12 +16,9 @@
 PAIRS = 4
 WIDE = 256
 CTX = 16
-STEPS = 2
+CHIPS = CTX // 2
+STEPS = 4
 TOKENS = SEG * LEN
-
-
-def owner_of(p, j):
-    return 2 * (2 * j + p % 2) + p // 2
 
 
 def kernel(
@@ -34,19 +31,34 @@
     stepP, uP, gP, xP, invP, decS,
     sumP, sumL, sumB,
     preP, preL, postP, postB,
-    send1, recv1, send2, recv2,
+    send1, recvC, send2, recv2, send3, recv3, sendS, entry,
     sIn, gIn, kpS,
     accQ, accK, accN,
     outI, outR, sendI, sendR,
     sums,
-    in_sem, s1_sem, r1_sem, s2_sem, r2_sem,
+    in_sem, c1_send, c1_recv, s2_sem, r2_sem, s3_sem, r3_sem, c4_send, c4_recv,
     hi_send, hi_recv, hr_send, hr_recv, own_sem, rs_send, rs_recv,
 ):
     me = lax.axis_index("ctx")
     hd = lax.axis_index("head")
     rows_out = TOKENS // heads
-    my_pair = 2 * lax.rem(me, 2) + lax.rem(me // 2, 2)
-    my_tile = my_pair * 4 + me // 4
+    chip = me // 2
+    core = lax.rem(me, 2)
+    sibling = me + 1 - 2 * core
+    near = chip // 4
+
+    def on_chip(d):
+        return 2 * lax.rem(chip + d, CHIPS) + core
+
+    barrier = pltpu.get_barrier_semaphore()
+    for d in sorted(range(1, CHIPS), key=lambda d: -min(d, CHIPS - d)):
+        pl.semaphore_signal(barrier, inc=1, device_id={"ctx": on_chip(d)}, device_id_type=MESH)
+    for d in range(1, heads):
+        pl.semaphore_signal(barrier, inc=1, device_id={"head": lax.rem(hd + d, heads)}, device_id_type=MESH)
+    pl.semaphore_signal(barrier, inc=1, device_id={"ctx": sibling}, device_id_type=MESH)
+
+    def first_order(it):
+        return 2 * lax.rem(core + 1 + it // 2, 2) + lax.rem(near + 1 + it, 2)
 
     k_copy = pltpu.make_async_copy(k_ref.at[0], kV, in_sem.at[3 * PAIRS])
     q_copy = pltpu.make_async_copy(q_ref.at[0], qV, in_sem.at[3 * PAIRS + 1])
@@ -55,18 +67,12 @@
 
     def in_copy(p, which):
         ref, buf = ((x_ref, xV), (rate_ref, rV), (g_ref, gV))[which]
-        lanes = pl.ds(p * WIDE, WIDE) if isinstance(p, int) else pl.ds(pl.multiple_of(p * WIDE, WIDE), WIDE)
+        lanes = pl.ds(pl.multiple_of(p * WIDE, WIDE), WIDE)
         return pltpu.make_async_copy(ref.at[0, :, lanes], buf.at[p], in_sem.at[p * 3 + which])
 
-    for p in range(PAIRS):
+    for it in range(PAIRS):
         for which in range(3):
-            in_copy(p, which).start()
-
-    barrier = pltpu.get_barrier_semaphore()
-    for d in range(1, CTX):
-        pl.semaphore_signal(barrier, inc=1, device_id={"ctx": lax.rem(me + d, CTX)}, device_id_type=MESH)
-    for d in range(1, heads):
-        pl.semaphore_signal(barrier, inc=1, device_id={"head": lax.rem(hd + d, heads)}, device_id_type=MESH)
+            in_copy(first_order(it), which).start()
 
     row = lax.broadcasted_iota(jnp.int32, (TOKENS, TOKENS), 0)
     col = lax.broadcasted_iota(jnp.int32, (TOKENS, TOKENS), 1)
@@ -93,43 +99,98 @@
     for i in range(LEN):
         knT[i] = norm[i * SEG:(i + 1) * SEG]
 
-    def to_owner(p, j):
-        o = owner_of(p, j)
-        return pltpu.make_async_remote_copy(
-            src_ref=send1.at[p * 4 + j], dst_ref=recv1.at[me], send_sem=s1_sem.at[p * 4 + j],
-            recv_sem=r1_sem.at[me], device_id={"ctx": o}, device_id_type=MESH)
-
-    def from_group(o):
-        return pltpu.make_async_remote_copy(
-            src_ref=send1.at[0], dst_ref=recv1.at[o], send_sem=s1_sem.at[0], recv_sem=r1_sem.at[o],
-            device_id={"ctx": o}, device_id_type=MESH)
-
-    def to_group(o):
-        return pltpu.make_async_remote_copy(
-            src_ref=send2.at[o], dst_ref=recv2.at[my_tile], send_sem=s2_sem.at[o], recv_sem=r2_sem.at[my_tile],
-            device_id={"ctx": o}, device_id_type=MESH)
-
-    def from_owner(p, j):
-        return pltpu.make_async_remote_copy(
-            src_ref=send2.at[0], dst_ref=recv2.at[p * 4 + j], send_sem=s2_sem.at[0],
-            recv_sem=r2_sem.at[p * 4 + j], device_id={"ctx": owner_of(p, j)}, device_id_type=MESH)
+    def to_sibling(p, a):
+        return pltpu.make_async_remote_copy(
+            src_ref=send1.at[pl.ds(p * 4, 4)], dst_ref=recvC.at[pl.ds(a * 4, 4)], send_sem=c1_send.at[a],
+            recv_sem=c1_recv.at[a], device_id={"ctx": sibling}, device_id_type=MESH)
+
+    def to_owner(t):
+        return pltpu.make_async_remote_copy(
+            src_ref=send2.at[t], dst_ref=recv2.at[chip], send_sem=s2_sem.at[t], recv_sem=r2_sem.at[chip],
+            device_id={"ctx": 2 * t + core}, device_id_type=MESH)
+
+    def from_chip(t):
+        return pltpu.make_async_remote_copy(
+            src_ref=send2.at[t], dst_ref=recv2.at[t], send_sem=s2_sem.at[t], recv_sem=r2_sem.at[t],
+            device_id={"ctx": 2 * t + core}, device_id_type=MESH)
+
+    def to_chip(t):
+        return pltpu.make_async_remote_copy(
+            src_ref=send3.at[t], dst_ref=recv3.at[chip], send_sem=s3_sem.at[t], recv_sem=r3_sem.at[chip],
+            device_id={"ctx": 2 * t + core}, device_id_type=MESH)
+
+    def from_owner(t):
+        return pltpu.make_async_remote_copy(
+            src_ref=send3.at[t], dst_ref=recv3.at[t], send_sem=s3_sem.at[t], recv_sem=r3_sem.at[t],
+            device_id={"ctx": 2 * t + core}, device_id_type=MESH)
+
+    def entries_out(p, a):
+        return pltpu.make_async_remote_copy(
+            src_ref=sendS.at[pl.ds(a * 4, 4)], dst_ref=entry.at[pl.ds(p * 4, 4)], send_sem=c4_send.at[a],
+            recv_sem=c4_recv.at[a], device_id={"ctx": sibling}, device_id_type=MESH)
+
+    def both(p, a, j, which):
+        mine = send1[p * 4 + j, which]
+        other = recvC[a * 4 + j, which]
+        return jnp.where(core == 0, mine, other), jnp.where(core == 0, other, mine)
+
+    def join(p, a):
+        to_sibling(p, a).wait_recv()
+        for j in range(4):
+            t = a * 4 + j
+            p0, p1 = both(p, a, j, 0)
+            l0, l1 = both(p, a, j, 1)
+            b0, b1 = both(p, a, j, 2)
+            send2[t, 0] = p0 * p1
+            send2[t, 1] = l0 * p1 + l1
+            send2[t, 2] = b0 + p0 * b1
+
+            @pl.when(t != chip)
+            def _():
+                to_owner(t).start()
+
+            @pl.when(t == chip)
+            def _():
+                recv2[t] = send2[t]
 
     def own_scan():
-        for d in range(1, CTX):
-            from_group(lax.rem(me + d, CTX)).wait_recv()
+        for d in range(1, CHIPS):
+            from_chip(lax.rem(chip + d, CHIPS)).wait_recv()
         state = jnp.zeros((SEG, LANES), F32)
         grad = state
-        for c in range(CTX):
-            send2[c, 0] = state
-            state = state * recv1[c, 0] + recv1[c, 1]
-        for c in reversed(range(CTX)):
-            send2[c, 1] = grad
-            grad = grad * recv1[c, 0] + recv1[c, 2]
-        for d in range(1, CTX):
-            to_group(lax.rem(me + d, CTX)).start()
-        recv2[my_tile] = send2[me]
-
-    def first_pass(p, _):
+        for c in range(CHIPS):
+            send3[c, 0] = state
+            state = state * recv2[c, 0] + recv2[c, 1]
+        for c in reversed(range(CHIPS)):
+            send3[c, 1] = grad
+            grad = grad * recv2[c, 0] + recv2[c, 2]
+        for d in sorted(range(1, CHIPS), key=lambda d: min(d, CHIPS - d)):
+            to_chip(lax.rem(chip + d, CHIPS)).start()
+        recv3[chip] = send3[chip]
+
+    def split(p, a):
+        for j in range(4):
+            t = a * 4 + j
+
+            @pl.when(t != chip)
+            def _():
+                from_owner(t).wait_recv()
+
+            s0 = recv3[t, 0]
+            g1 = recv3[t, 1]
+            p0, p1 = both(p, a, j, 0)
+            l0, _ = both(p, a, j, 1)
+            _, b1 = both(p, a, j, 2)
+            s1 = s0 * p0 + l0
+            g0 = g1 * p1 + b1
+            entry[p * 4 + j, 0] = jnp.where(core == 0, s0, s1)
+            entry[p * 4 + j, 1] = jnp.where(core == 0, g0, g1)
+            sendS[t, 0] = jnp.where(core == 0, s1, s0)
+            sendS[t, 1] = jnp.where(core == 0, g1, g0)
+        entries_out(p, a).start()
+
+    def first_pass(it, _):
+        p = first_order(it)
         for which in range(3):
             in_copy(p, which).wait()
         for c in range(2):
@@ -215,22 +276,17 @@
                 run_p = run_p * ps[s]
             send1[o, 2] = run_b
 
-        @pl.when(p == 0)
+        a = lax.rem(near + 1 + it, 2)
+
+        @pl.when(it == 1)
         def _():
-            pl.semaphore_wait(barrier, CTX - 1 + heads - 1)
-
-        for j in range(4):
-            @pl.when(owner_of(p, j) != me)
-            def _():
-                to_owner(p, j).start()
-
-            @pl.when(owner_of(p, j) == me)
-            def _():
-                recv1[me] = send1[p * 4 + j]
-
-        @pl.when((p >= 2) & (my_pair == p - 2))
+            pl.semaphore_wait(barrier, CHIPS + heads - 1)
+            for b in range(2):
+                to_sibling(2 * (1 - core) + b, b).start()
+
+        @pl.when(it >= 2)
         def _():
-            own_scan()
+            join(p, a)
         return 0
 
     lax.fori_loop(0, PAIRS, first_pass, 0)
@@ -246,9 +302,7 @@
 
     lax.fori_loop(0, LEN, clear, 0)
 
-    @pl.when(my_pair == 2)
-    def _():
-        own_scan()
+    own_scan()
 
     def head_copy(p, h, owner, src_buf, dst, ssem, rsem):
         return pltpu.make_async_remote_copy(
@@ -265,17 +319,23 @@
 
     arrays = ((sendI, oi_ref, hi_send, hi_recv), (sendR, or_ref, hr_send, hr_recv))
 
-    def second_pass(p, _):
+    def second_pass(it, _):
+        a = lax.rem(near + it, 2)
+        p = 2 * lax.rem(core + it // 2, 2) + a
         base = p * (2 * LEN)
+
+        @pl.when(it < 2)
+        def _():
+            split(p, a)
+
+        @pl.when(it >= 2)
+        def _():
+            entries_out(p, a).wait_recv()
+
         for j in range(4):
             o = p * 4 + j
-
-            @pl.when(owner_of(p, j) != me)
-            def _():
-                from_owner(p, j).wait_recv()
-
-            s0 = recv2[o, 0]
-            g0 = recv2[o, 1]
+            s0 = entry[o, 0]
+            g0 = entry[o, 1]
             tile = j * 8 * SEG
             for s in range(SEG):
                 at = o * SEG + s
@@ -356,10 +416,6 @@
                 head_copy(p, lax.rem(hd + d, heads), hd, src_buf, dst, ssem, rsem).start()
         own_copy(p, 0, sendI, oi_ref).start()
         own_copy(p, 1, sendR, or_ref).start()
-
-        @pl.when((p == 0) & (my_pair == 3))
-        def _():
-            own_scan()
         return 0
 
     lax.fori_loop(0, PAIRS, second_pass, 0)
@@ -389,13 +445,12 @@
         sum_copy(lax.rem(hd + d, heads), hd).start()
     rs_ref[hd] = sums[pl.ds(pl.multiple_of(hd * rows_out, rows_out), rows_out), :]
 
-    for p in range(PAIRS):
-        for j in range(4):
-            @pl.when(owner_of(p, j) != me)
-            def _():
-                to_owner(p, j).wait_send()
-    for d in range(1, CTX):
-        to_group(lax.rem(me + d, CTX)).wait_send()
+    for d in range(1, CHIPS):
+        to_owner(lax.rem(chip + d, CHIPS)).wait_send()
+        to_chip(lax.rem(chip + d, CHIPS)).wait_send()
+    for a in range(2):
+        to_sibling(a, a).wait_send()
+        entries_out(a, a).wait_send()
     for p in range(PAIRS):
         own_copy(p, 0, sendI, oi_ref).wait()
         own_copy(p, 1, sendR, or_ref).wait()
@@ -464,7 +519,8 @@
                 regs(PAIRS * LEN * 2 * N),
                 *[pltpu.VMEM((2 * N * SEG, LANES), F32) for _ in range(3)],
                 *[regs(CTX * SEG) for _ in range(4)],
-                regs(CTX, 3), regs(CTX, 3), regs(CTX, 2), regs(CTX, 2),
+                regs(CTX, 3), regs(CHIPS, 3), regs(CHIPS, 3), regs(CHIPS, 3),
+                regs(CHIPS, 2), regs(CHIPS, 2), regs(CHIPS, 2), regs(CTX, 2),
                 pltpu.VMEM((2 * N * SEG, LANES), F32), pltpu.VMEM((2 * N * SEG, LANES), F32),
                 regs(LEN * 2 * N),
                 regs(LEN * N), regs(LEN * N), regs(LEN),
@@ -472,7 +528,7 @@
                 pltpu.VMEM((PAIRS, TOKENS, WIDE), BF16), pltpu.VMEM((PAIRS, TOKENS, WIDE), BF16),
                 pltpu.VMEM((TOKENS, LANES), F32),
                 dma((3 * PAIRS + 2,)),
-                dma((CTX,)), dma((CTX,)), dma((CTX,)), dma((CTX,)),
+                dma((2,)), dma((2,)), *[dma((CHIPS,)) for _ in range(4)], dma((2,)), dma((2,)),
                 dma((PAIRS, heads)), dma((PAIRS, heads)), dma((PAIRS, heads)), dma((PAIRS, heads)),
                 dma((PAIRS, 2)), dma((heads,)), dma((heads,)),
             ],

time: 34.8 us -> 32.5 us (0.934)
  the two profiles are of different devices: /device:TPU:1 before, /device:TPU:6 now
where the time goes in v2:
time: 32.5 us; the launch traced here: 32.3 us
  Pallas kernels  31.7 us (98%)
  between operations  0.64 us (2%)
    pallas_call x1, Pallas kernels, run(): pl.pallas_call(lambda *refs: kernel(heads, *refs), out_shape=(pltpu.VMEM(...  30.9 us
    pallas_call x1, Pallas kernels, run(): pl.pallas_call(lambda *refs: finish(heads, *refs), out_shape=(wide, wide,...  0.83 us

profile of v2, /device:TPU:6, one launch (start us, length us, event | category | flops | bytes accessed | tf_op | source)
XLA Modules:
  0.0 32.3 jit_solution(2724965547876904862)
XLA Ops:
  0.6 30.9 %shard_map.84 = (bf16[1,32,4096]{2,1,0:T(8,128)(2,1)S(1)}, bf16[1,32,4096]{2,1,0:T(8,128)(2,1)S(1)}, f32[4,32,128]{2,1,0:T(8,128)S(1)}) custom-call(bf16[1,128,1024]{2,1,0:T(8,128)(2,1)} %refs_0_.1, f32[1,128,1024]{2,1,0:T(8,128)} %refs_1_.1, bf16[1,16,128]{2,1,0:T(8,128)(2,1)} %bitcast.4, bf16[1,16,128]{2,1,0:T(8,128)(2,1)} %bitcast.5, ...), custom_call_target="tpu_custom_call" | custom-call | tf_op jit(solution)/shard_map/pallas_call | solution.py:503
  31.5 0.8 %shard_map.85 = (bf16[1,32,4096]{2,1,0:T(8,128)(2,1)}, bf16[1,32,4096]{2,1,0:T(8,128)(2,1)}, f32[1,16,32]{2,1,0:T(8,128)}, f32[1,16,32]{2,1,0:T(8,128)}) custom-call(bf16[1,32,4096]{2,1,0:T(8,128)(2,1)S(1)} %get-tuple-element.11.refs_0_, bf16[1,32,4096]{2,1,0:T(8,128)(2,1)S(1)} %get-tuple-element.12.refs_1_, f32[4,32,128]{2,1,0:T(8,128)S(1)} %get-tuple-element.13.refs_2_), custom_call_target="tpu_custom_call" | custom-call | tf_op jit(solution)/shard_map/pallas_call | solution.py:541

commit v3 on v2

--- a/solution.py
+++ b/solution.py
@@ -24,20 +24,20 @@
 def kernel(
     heads,
     x_ref, rate_ref, k_ref, q_ref, g_ref,
-    oi_ref, or_ref, rs_ref,
+    o_ref, rs_ref,
     xV, rV, gV, kV, qV,
     kT, k2T, qT, knT, kL,
     x32, g32, r32,
-    stepP, uP, gP, xP, invP, decS,
+    stepP, uP, gP, xP, invP, decS, driveS, emitS,
     sumP, sumL, sumB,
     preP, preL, postP, postB,
     send1, recvC, send2, recv2, send3, recv3, sendS, entry,
     sIn, gIn, kpS,
     accQ, accK, accN,
-    outI, outR, sendI, sendR,
+    outI, outR, sendB,
     sums,
     in_sem, c1_send, c1_recv, s2_sem, r2_sem, s3_sem, r3_sem, c4_send, c4_recv,
-    hi_send, hi_recv, hr_send, hr_recv, own_sem, rs_send, rs_recv,
+    h_send, h_recv, own_sem, rs_send, rs_recv,
 ):
     me = lax.axis_index("ctx")
     hd = lax.axis_index("head")
@@ -61,7 +61,7 @@
         return 2 * lax.rem(core + 1 + it // 2, 2) + lax.rem(near + 1 + it, 2)
 
     k_copy = pltpu.make_async_copy(k_ref.at[0], kV, in_sem.at[3 * PAIRS])
-    q_copy = pltpu.make_async_copy(q_ref.at[0], qV, in_sem.at[3 * PAIRS + 1])
+    q_copy = pltpu.make_async_copy(q_ref.at[0], qV, in_sem.at[3 * PAIRS])
     k_copy.start()
     q_copy.start()
 
@@ -304,22 +304,56 @@
 
     own_scan()
 
-    def head_copy(p, h, owner, src_buf, dst, ssem, rsem):
-        return pltpu.make_async_remote_copy(
-            src_ref=src_buf.at[p, pl.ds(pl.multiple_of(h * rows_out, rows_out), rows_out), :],
-            dst_ref=dst.at[0, :, pl.ds(pl.multiple_of(owner * (PAIRS * WIDE) + p * WIDE, WIDE), WIDE)],
-            send_sem=ssem.at[p, h], recv_sem=rsem.at[p, owner],
+    def fill(at, _):
+        i = lax.rem(at, LEN)
+        u = [uP[2 * at + c] for c in range(2)]
+        gv = [gP[2 * at + c] for c in range(2)]
+        for n in range(N):
+            kk = kT[i * N + n]
+            qq = qT[i * N + n]
+            for c in range(2):
+                driveS[at * (2 * N) + 2 * n + c] = u[c] * kk
+                emitS[at * (2 * N) + 2 * n + c] = gv[c] * qq
+        return 0
+
+    lax.fori_loop(0, PAIRS * LEN, fill, 0)
+
+    def pair_at(it):
+        return 2 * lax.rem(core + it // 2, 2) + lax.rem(near + it, 2)
+
+    def part_lanes(p, c):
+        return (pl.ds(0, WIDE), p * WIDE, WIDE) if c is None else (
+            pl.ds(pl.multiple_of(c * LANES, LANES), LANES), p * WIDE + c * LANES, LANES)
+
+    def head_copy(slot, p, c, h, owner):
+        lanes, column, width = part_lanes(p, c)
+        return pltpu.make_async_remote_copy(
+            src_ref=sendB.at[p, :, pl.ds(pl.multiple_of(h * rows_out, rows_out), rows_out), lanes],
+            dst_ref=o_ref.at[:, :, pl.ds(pl.multiple_of(owner * (PAIRS * WIDE) + column, width), width)],
+            send_sem=h_send.at[slot, h], recv_sem=h_recv.at[slot, owner],
             device_id={"head": h}, device_id_type=MESH)
 
-    def own_copy(p, which, src_buf, dst):
+    def own_copy(slot, p, c):
+        lanes, column, width = part_lanes(p, c)
         return pltpu.make_async_copy(
-            src_buf.at[p, pl.ds(pl.multiple_of(hd * rows_out, rows_out), rows_out), :],
-            dst.at[0, :, pl.ds(pl.multiple_of(hd * (PAIRS * WIDE) + p * WIDE, WIDE), WIDE)],
-            own_sem.at[p, which])
-
-    arrays = ((sendI, oi_ref, hi_send, hi_recv), (sendR, or_ref, hr_send, hr_recv))
-
-    def second_pass(it, _):
+            sendB.at[p, :, pl.ds(pl.multiple_of(hd * rows_out, rows_out), rows_out), lanes],
+            o_ref.at[:, :, pl.ds(pl.multiple_of(hd * (PAIRS * WIDE) + column, width), width)],
+            own_sem.at[slot])
+
+    def ship(slot, p, c):
+        for d in sorted(range(1, heads), key=lambda d: -min(d, heads - d)):
+            head_copy(slot, p, c, lax.rem(hd + d, heads), hd).start()
+        own_copy(slot, p, c).start()
+
+    def shipped(slot, p, c):
+        own_copy(slot, p, c).wait()
+        for d in range(1, heads):
+            h = lax.rem(hd + d, heads)
+            copy = head_copy(slot, p, c, h, h)
+            copy.wait_send()
+            copy.wait_recv()
+
+    def second_pass(it):
         a = lax.rem(near + it, 2)
         p = 2 * lax.rem(core + it // 2, 2) + a
         base = p * (2 * LEN)
@@ -342,83 +376,87 @@
                 sIn[pl.ds(tile + s, SEG, stride=SEG), :] = preP[at] * s0 + preL[at]
                 gIn[pl.ds(tile + s, SEG, stride=SEG), :] = postP[at] * g0 + postB[at]
 
+        return p, base
+
+    def grads_of(p, base, chunks):
+        width = len(chunks)
+
         def forward(i, states):
             states = list(states)
-            u = [uP[base + 2 * i + c] for c in range(2)]
-            gv = [gP[base + 2 * i + c] for c in range(2)]
+            gv = [gP[base + 2 * i + c] for c in chunks]
             for n in range(N):
                 kk = kT[i * N + n]
                 total = accQ[i * N + n]
-                for c in range(2):
-                    j = n * 2 + c
+                for b, c in enumerate(chunks):
+                    j = n * width + b
                     kpS[i * (2 * N) + j] = kk * states[j]
-                    states[j] = decS[(p * LEN + i) * (2 * N) + j] * states[j] + u[c] * kk
-                    total = total + gv[c] * states[j]
+                    states[j] = decS[(p * LEN + i) * (2 * N) + 2 * n + c] * states[j] + driveS[(p * LEN + i) * (2 * N) + 2 * n + c]
+                    total = total + gv[b] * states[j]
                 accQ[i * N + n] = total
             return tuple(states)
 
-        start = tuple(sIn[pl.ds((c * N + n) * SEG, SEG), :] for n in range(N) for c in range(2))
         def forward_some(b, states):
             for r in range(STEPS):
                 states = forward(b * STEPS + r, states)
             return states
 
-        lax.fori_loop(0, LEN // STEPS, forward_some, start)
+        def start(ref):
+            return tuple(
+                ref[pl.ds(pl.multiple_of((c * N + n) * SEG, SEG), SEG), :] for n in range(N) for c in chunks)
+
+        lax.fori_loop(0, LEN // STEPS, forward_some, start(sIn))
 
         def backward(it2, grads):
             i = LEN - 1 - it2
             grads = list(grads)
-            step = [stepP[base + 2 * i + c] for c in range(2)]
+            step = [stepP[base + 2 * i + c] for c in chunks]
             twice = [s + s for s in step]
-            u = [uP[base + 2 * i + c] for c in range(2)]
-            gv = [gP[base + 2 * i + c] for c in range(2)]
-            key_dot = [None, None]
-            weighted = [None, None]
+            u = [uP[base + 2 * i + c] for c in chunks]
+            key_dot = [None] * width
+            weighted = [None] * width
             for n in range(N):
                 kk = kT[i * N + n]
-                qq = qT[i * N + n]
                 total = accK[i * N + n]
-                for c in range(2):
-                    j = n * 2 + c
+                for b, c in enumerate(chunks):
+                    j = n * width + b
                     kprev = kpS[i * (2 * N) + j]
-                    grad = grads[j] + gv[c] * qq
+                    grad = grads[j] + emitS[(p * LEN + i) * (2 * N) + 2 * n + c]
                     gk = grad * kk
                     wk = gk * kprev
-                    key_dot[c] = gk if n == 0 else key_dot[c] + gk
-                    weighted[c] = wk if n == 0 else weighted[c] + wk
-                    total = total + grad * (u[c] - twice[c] * kprev)
-                    grads[j] = grad * decS[(p * LEN + i) * (2 * N) + j]
+                    key_dot[b] = gk if n == 0 else key_dot[b] + gk
+                    weighted[b] = wk if n == 0 else weighted[b] + wk
+                    total = total + grad * (u[b] - twice[b] * kprev)
+                    grads[j] = grad * decS[(p * LEN + i) * (2 * N) + 2 * n + c]
                 accK[i * N + n] = total
             norm_sum = accN[i]
-            for c in range(2):
+            for b, c in enumerate(chunks):
                 at = base + 2 * i + c
                 inv = invP[at]
-                outI[c, pl.ds(i, SEG, stride=LEN), :] = step[c] * key_dot[c]
-                grad_step = xP[at] * key_dot[c] - weighted[c]
-                outR[c, pl.ds(i, SEG, stride=LEN), :] = grad_step * (inv * inv)
-                norm_sum = norm_sum + grad_step * (step[c] * step[c])
+                outI[b, pl.ds(i, SEG, stride=LEN), :] = step[b] * key_dot[b]
+                grad_step = xP[at] * key_dot[b] - weighted[b]
+                outR[b, pl.ds(i, SEG, stride=LEN), :] = grad_step * (inv * inv)
+                norm_sum = norm_sum + grad_step * (step[b] * step[b])
             accN[i] = norm_sum
             return tuple(grads)
 
-        start = tuple(gIn[pl.ds((c * N + n) * SEG, SEG), :] for n in range(N) for c in range(2))
         def backward_some(b, grads):
             for r in range(STEPS):
                 grads = backward(b * STEPS + r, grads)
             return grads
 
-        lax.fori_loop(0, LEN // STEPS, backward_some, start)
-        for c in range(2):
-            lanes = pl.ds(c * LANES, LANES)
-            sendI[p, :, lanes] = outI[c].astype(BF16)
-            sendR[p, :, lanes] = outR[c].astype(BF16)
-        for d in range(1, heads):
-            for src_buf, dst, ssem, rsem in arrays:
-                head_copy(p, lax.rem(hd + d, heads), hd, src_buf, dst, ssem, rsem).start()
-        own_copy(p, 0, sendI, oi_ref).start()
-        own_copy(p, 1, sendR, or_ref).start()
+        lax.fori_loop(0, LEN // STEPS, backward_some, start(gIn))
+        for b, c in enumerate(chunks):
+            lanes = pl.ds(c * LANES, LANES) if isinstance(c, int) else pl.ds(pl.multiple_of(c * LANES, LANES), LANES)
+            sendB[p, 0, :, lanes] = outI[b].astype(BF16)
+            sendB[p, 1, :, lanes] = outR[b].astype(BF16)
+
+    def pair_grads(it, _):
+        p, base = second_pass(it)
+        grads_of(p, base, (0, 1))
+        ship(it, p, None)
         return 0
 
-    lax.fori_loop(0, PAIRS, second_pass, 0)
+    lax.fori_loop(0, PAIRS, pair_grads, 0)
 
     ones = jnp.ones((2 * LANES, LANES), BF16)
     lane = lax.broadcasted_iota(jnp.int32, (TOKENS, LANES), 1)
@@ -451,15 +489,8 @@
     for a in range(2):
         to_sibling(a, a).wait_send()
         entries_out(a, a).wait_send()
-    for p in range(PAIRS):
-        own_copy(p, 0, sendI, oi_ref).wait()
-        own_copy(p, 1, sendR, or_ref).wait()
-        for d in range(1, heads):
-            h = lax.rem(hd + d, heads)
-            for src_buf, dst, ssem, rsem in arrays:
-                copy = head_copy(p, h, h, src_buf, dst, ssem, rsem)
-                copy.wait_send()
-                copy.wait_recv()
+    for it in range(PAIRS):
+        shipped(it, pair_at(it), None)
     for d in range(1, heads):
         h = lax.rem(hd + d, heads)
         copy = sum_copy(h, h)
@@ -467,9 +498,9 @@
         copy.wait_recv()
 
 
-def finish(heads, i_ref, r_ref, s_ref, oi_ref, or_ref, ok_ref, oq_ref, small, sem):
-    first = pltpu.make_async_copy(i_ref, oi_ref, sem.at[0])
-    second = pltpu.make_async_copy(r_ref, or_ref, sem.at[1])
+def finish(heads, b_ref, s_ref, oi_ref, or_ref, ok_ref, oq_ref, small, sem):
+    first = pltpu.make_async_copy(b_ref.at[pl.ds(0, 1)], oi_ref, sem.at[0])
+    second = pltpu.make_async_copy(b_ref.at[pl.ds(1, 1)], or_ref, sem.at[1])
     first.start()
     second.start()
     total = s_ref[0]
@@ -500,15 +531,14 @@
         dma = pltpu.SemaphoreType.DMA
         wide = jax.ShapeDtypeStruct((1, rows_out, width), BF16)
         small = jax.ShapeDtypeStruct((1, N, rows_out), F32)
-        grads_in, grads_rate, partial = pl.pallas_call(
+        grads, partial = pl.pallas_call(
             lambda *refs: kernel(heads, *refs),
             out_shape=(
-                pltpu.VMEM((1, rows_out, width), BF16),
-                pltpu.VMEM((1, rows_out, width), BF16),
+                pltpu.VMEM((2, rows_out, width), BF16),
                 pltpu.VMEM((heads, rows_out, LANES), F32),
             ),
             in_specs=[hbm] * 5,
-            out_specs=(vmem, vmem, vmem),
+            out_specs=(vmem, vmem),
             scratch_shapes=[
                 pltpu.VMEM((PAIRS, TOKENS, WIDE), BF16), pltpu.VMEM((PAIRS, TOKENS, WIDE), F32),
                 pltpu.VMEM((PAIRS, TOKENS, WIDE), BF16),
@@ -516,6 +546,8 @@
                 regs(LEN * N), regs(LEN * N), regs(LEN * N), regs(LEN), pltpu.VMEM((TOKENS, LANES), F32),
                 *[pltpu.VMEM((2, TOKENS, LANES), F32) for _ in range(3)],
                 *[regs(PAIRS * 2 * LEN) for _ in range(5)],
+                regs(PAIRS * LEN * 2 * N),
+                regs(PAIRS * LEN * 2 * N),
                 regs(PAIRS * LEN * 2 * N),
                 *[pltpu.VMEM((2 * N * SEG, LANES), F32) for _ in range(3)],
                 *[regs(CTX * SEG) for _ in range(4)],
@@ -525,12 +557,11 @@
                 regs(LEN * 2 * N),
                 regs(LEN * N), regs(LEN * N), regs(LEN),
                 pltpu.VMEM((2, TOKENS, LANES), F32), pltpu.VMEM((2, TOKENS, LANES), F32),
-                pltpu.VMEM((PAIRS, TOKENS, WIDE), BF16), pltpu.VMEM((PAIRS, TOKENS, WIDE), BF16),
+                pltpu.VMEM((PAIRS, 2, TOKENS, WIDE), BF16),
                 pltpu.VMEM((TOKENS, LANES), F32),
                 dma((3 * PAIRS + 2,)),
                 dma((2,)), dma((2,)), *[dma((CHIPS,)) for _ in range(4)], dma((2,)), dma((2,)),
-                dma((PAIRS, heads)), dma((PAIRS, heads)), dma((PAIRS, heads)), dma((PAIRS, heads)),
-                dma((PAIRS, 2)), dma((heads,)), dma((heads,)),
+                dma((PAIRS, heads)), dma((PAIRS, heads)), dma((PAIRS,)), dma((heads,)), dma((heads,)),
             ],
             compiler_params=pltpu.CompilerParams(
                 collective_id=0, has_side_effects=True, vmem_limit_bytes=48 * 1024 * 1024),
@@ -541,10 +572,10 @@
         grads_in, grads_rate, keys, queries = pl.pallas_call(
             lambda *refs: finish(heads, *refs),
             out_shape=(wide, wide, small, small),
-            in_specs=[vmem, vmem, vmem],
+            in_specs=[vmem, vmem],
             out_specs=(hbm, hbm, hbm, hbm),
             scratch_shapes=[pltpu.VMEM((2, N, rows_out), F32), dma((4,))],
-        )(*(pltpu.with_memory_space_constraint(a, pltpu.VMEM) for a in (grads_in, grads_rate, partial)))
+        )(*(pltpu.with_memory_space_constraint(a, pltpu.VMEM) for a in (grads, partial)))
         return grads_in, grads_rate, jnp.swapaxes(keys, 1, 2), jnp.swapaxes(queries, 1, 2)
 
     return run

time: 32.5 us -> 31.5 us (0.969)
  Pallas kernels: 31.7 us -> 30.7 us
    pallas_call x1, Pallas kernels: 30.9 us -> 29.9 us  [run(): pl.pallas_call(lambda *refs: kernel(heads, *refs), out_shape=(pltpu.VMEM(...]
where the time goes in v3:
time: 31.5 us; the launch traced here: 31.4 us
  Pallas kernels  30.7 us (97%)
  between operations  0.64 us (2%)
    pallas_call x1, Pallas kernels, run(): pl.pallas_call(lambda *refs: kernel(heads, *refs), out_shape=(pltpu.VMEM(...  29.9 us
    pallas_call x1, Pallas kernels, run(): pl.pallas_call(lambda *refs: finish(heads, *refs), out_shape=(wide, wide,...  0.83 us

profile of v3, /device:TPU:6, one launch (start us, length us, event | category | flops | bytes accessed | tf_op | source)
XLA Modules:
  0.0 31.4 jit_solution(3750224619041341674)
XLA Ops:
  0.6 29.9 %shard_map.84 = (bf16[2,32,4096]{2,1,0:T(8,128)(2,1)S(1)}, f32[4,32,128]{2,1,0:T(8,128)S(1)}) custom-call(bf16[1,128,1024]{2,1,0:T(8,128)(2,1)} %refs_0_.1, f32[1,128,1024]{2,1,0:T(8,128)} %refs_1_.1, bf16[1,16,128]{2,1,0:T(8,128)(2,1)} %bitcast.4, bf16[1,16,128]{2,1,0:T(8,128)(2,1)} %bitcast.5, bf16[1,128,1024]{2,1,0:T(8,128)(2,1)} %refs_4_.1), custom_call_target="tpu_custom_call" | custom-call | tf_op jit(solution)/shard_map/pallas_call | solution.py:534
  30.6 0.8 %shard_map.85 = (bf16[1,32,4096]{2,1,0:T(8,128)(2,1)}, bf16[1,32,4096]{2,1,0:T(8,128)(2,1)}, f32[1,16,32]{2,1,0:T(8,128)}, f32[1,16,32]{2,1,0:T(8,128)}) custom-call(bf16[2,32,4096]{2,1,0:T(8,128)(2,1)S(1)} %get-tuple-element.10.refs_0_, f32[4,32,128]{2,1,0:T(8,128)S(1)} %get-tuple-element.11.refs_1_), custom_call_target="tpu_custom_call" | custom-call | tf_op jit(solution)/shard_map/pallas_call | solution.py:572

commit v4 on v3

--- a/solution.py
+++ b/solution.py
@@ -35,7 +35,7 @@
     sIn, gIn, kpS,
     accQ, accK, accN,
     outI, outR, sendB,
-    sums,
+    sums, packS,
     in_sem, c1_send, c1_recv, s2_sem, r2_sem, s3_sem, r3_sem, c4_send, c4_recv,
     h_send, h_recv, own_sem, rs_send, rs_recv,
 ):
@@ -474,14 +474,25 @@
     for i in range(LEN):
         sums[pl.ds(i, SEG, stride=LEN), :] = merged[i * SEG:(i + 1) * SEG]
 
+    turned = sums[...].T
+    quarter = lax.broadcasted_iota(jnp.int32, (SEG, LANES), 1) // rows_out
+    for h in range(heads):
+        packed = zero
+        for q in range(2 * N // SEG):
+            moved = turned[q * SEG:(q + 1) * SEG]
+            if q != h:
+                moved = pltpu.roll(moved, (rows_out * (q - h)) % LANES, 1)
+            packed = jnp.where(quarter == q, moved, packed)
+        packS[h] = packed
+
     def sum_copy(h, src):
         return pltpu.make_async_remote_copy(
-            src_ref=sums.at[pl.ds(pl.multiple_of(h * rows_out, rows_out), rows_out), :], dst_ref=rs_ref.at[src], send_sem=rs_send.at[h], recv_sem=rs_recv.at[src],
+            src_ref=packS.at[h], dst_ref=rs_ref.at[src], send_sem=rs_send.at[h], recv_sem=rs_recv.at[src],
             device_id={"head": h}, device_id_type=MESH)
 
     for d in range(1, heads):
         sum_copy(lax.rem(hd + d, heads), hd).start()
-    rs_ref[hd] = sums[pl.ds(pl.multiple_of(hd * rows_out, rows_out), rows_out), :]
+    rs_ref[hd] = packS[hd]
 
     for d in range(1, CHIPS):
         to_owner(lax.rem(chip + d, CHIPS)).wait_send()
@@ -506,9 +517,9 @@
     total = s_ref[0]
     for h in range(1, heads):
         total = total + s_ref[h]
-    turned = total.T
-    small[0] = turned[:N]
-    small[1] = turned[N:2 * N]
+    rows_out = TOKENS // heads
+    for q in range(2 * N // SEG):
+        small[q // 2, (q % 2) * SEG:(q % 2 + 1) * SEG, :] = total[:, q * rows_out:(q + 1) * rows_out]
     third = pltpu.make_async_copy(small.at[0], ok_ref.at[0], sem.at[2])
     fourth = pltpu.make_async_copy(small.at[1], oq_ref.at[0], sem.at[3])
     third.start()
@@ -535,7 +546,7 @@
             lambda *refs: kernel(heads, *refs),
             out_shape=(
                 pltpu.VMEM((2, rows_out, width), BF16),
-                pltpu.VMEM((heads, rows_out, LANES), F32),
+                pltpu.VMEM((heads, SEG, LANES), F32),
             ),
             in_specs=[hbm] * 5,
             out_specs=(vmem, vmem),
@@ -558,7 +569,7 @@
                 regs(LEN * N), regs(LEN * N), regs(LEN),
                 pltpu.VMEM((2, TOKENS, LANES), F32), pltpu.VMEM((2, TOKENS, LANES), F32),
                 pltpu.VMEM((PAIRS, 2, TOKENS, WIDE), BF16),
-                pltpu.VMEM((TOKENS, LANES), F32),
+                pltpu.VMEM((TOKENS, LANES), F32), regs(heads),
                 dma((3 * PAIRS + 2,)),
                 dma((2,)), dma((2,)), *[dma((CHIPS,)) for _ in range(4)], dma((2,)), dma((2,)),
                 dma((PAIRS, heads)), dma((PAIRS, heads)), dma((PAIRS,)), dma((heads,)), dma((heads,)),

time: 31.5 us -> 31.4 us (level)
  no operation moved by 1% of the time
where the time goes in v4:
time: 31.4 us; the launch traced here: 31.3 us
  Pallas kernels  30.6 us (97%)
  between operations  0.64 us (2%)
    pallas_call x1, Pallas kernels, run(): pl.pallas_call(lambda *refs: kernel(heads, *refs), out_shape=(pltpu.VMEM(...  29.8 us
    pallas_call x1, Pallas kernels, run(): pl.pallas_call(lambda *refs: finish(heads, *refs), out_shape=(wide, wide,...  0.83 us

profile of v4, /device:TPU:6, one launch (start us, length us, event | category | flops | bytes accessed | tf_op | source)
XLA Modules:
  0.0 31.3 jit_solution(4169299642522462318)
XLA Ops:
  0.6 29.8 %shard_map.84 = (bf16[2,32,4096]{2,1,0:T(8,128)(2,1)S(1)}, f32[4,8,128]{2,1,0:T(8,128)S(1)}) custom-call(bf16[1,128,1024]{2,1,0:T(8,128)(2,1)} %refs_0_.1, f32[1,128,1024]{2,1,0:T(8,128)} %refs_1_.1, bf16[1,16,128]{2,1,0:T(8,128)(2,1)} %bitcast.4, bf16[1,16,128]{2,1,0:T(8,128)(2,1)} %bitcast.5, bf16[1,128,1024]{2,1,0:T(8,128)(2,1)} %refs_4_.1), custom_call_target="tpu_custom_call" | custom-call | tf_op jit(solution)/shard_map/pallas_call | solution.py:545
  30.5 0.8 %shard_map.85 = (bf16[1,32,4096]{2,1,0:T(8,128)(2,1)}, bf16[1,32,4096]{2,1,0:T(8,128)(2,1)}, f32[1,16,32]{2,1,0:T(8,128)}, f32[1,16,32]{2,1,0:T(8,128)}) custom-call(bf16[2,32,4096]{2,1,0:T(8,128)(2,1)S(1)} %get-tuple-element.10.refs_0_, f32[4,8,128]{2,1,0:T(8,128)S(1)} %get-tuple-element.11.refs_1_), custom_call_target="tpu_custom_call" | custom-call | tf_op jit(solution)/shard_map/pallas_call | solution.py:583
